TPU v7x, 32 devices: a whole 2x2x4 slice. The times are simulated.
32 devices in a mesh: row: 4 (over y, x), col: 2 (over core), depth: 4 (over z).
Axes of the slice: x: 2, y: 2, z: 4, core: 2. Of those that a mesh axis runs over, the one named last changes fastest.
Arguments:
- x_vals: bfloat16 [4, 16, 4, 128, 128], P('row', ('col', 'depth')), may hold values from -2.5 to 2.5
- x_rows: int32 [4, 16, 4], P('row', ('col', 'depth')), may hold values from -1 to 3, as said below
- out_block: int32 [4, 2, 4], P('row', 'col', 'depth'), may hold values from 0 to 15, as said below
Outputs:
- product_blocks: bfloat16 [4, 2, 4, 128, 128], P('row', 'col', 'depth')
Inputs may be any that keep to these rules, and one draw needn't show every extreme that they name: `x_rows`: within one row group and block column the filled slots name distinct rows. In every row group, each run of 2 block columns that starts at a multiple of 2 has a column with all 4 slots filled. `out_block`: within one tile the 4 entries are distinct positions, and every tile lists position 15 among them.
All inputs are finite; a program needn't handle non-finite values.
Results may differ from a plain program's by a relative error of at most 0.001.
Values may be sent and summed in bfloat16 or wider, within the bound.
A program may use at most 128 MiB of HBM per device.

v0:
```python
import functools

import jax
import jax.numpy as jnp
from jax import lax
from jax.experimental import pallas as pl
from jax.experimental.pallas import tpu as pltpu
from jax.sharding import PartitionSpec as P

MESH = pl.DeviceIdType.MESH
CHUNKS = 4
VMEM_LIMIT = 64 * 1024 * 1024


def product(left, right):
    return lax.dot_general(
        left, right, (((1,), (1,)), ((), ())), preferred_element_type=jnp.float32
    )


def kernel(
    sizes, rows_hbm, pos_ref, x_ref, out_ref,
    home, home_rows, partner, partner_rows, rows_smem, pos_vmem,
    left, send_parts, recv_parts,
    local_sem, home_send, home_recv, partner_send, partner_recv,
    row_send, row_recv, pos_send, pos_recv, sum_send, sum_recv,
):
    row_count, col_count, depth_count = sizes
    width, slots, size = x_ref.shape[1], x_ref.shape[2], x_ref.shape[3]
    chunks, sub = len(partner), partner[0].shape[3]
    group_rows = width * col_count * depth_count // row_count
    midpoint = col_count // 2
    row, col, depth = (lax.axis_index(name) for name in ("row", "col", "depth"))
    has_partner = col != midpoint

    def place(row_index, col_index, depth_index):
        return {"row": row_index, "col": col_index, "depth": depth_index}

    loads = [
        pltpu.make_async_copy(x_ref.at[0], home.at[0], local_sem.at[0]),
        pltpu.make_async_copy(rows_hbm.at[0], home_rows.at[0], local_sem.at[1]),
        pltpu.make_async_copy(pos_ref.at[0], pos_vmem.at[0], local_sem.at[2]),
    ]
    for copy in loads:
        copy.start()

    barrier = pltpu.get_barrier_semaphore()

    def greet(device):
        pl.semaphore_signal(barrier, inc=1, device_id=device, device_id_type=MESH)

    for step in range(1, col_count):
        greet(place(row, lax.rem(col + step, col_count), depth))
    for step in range(1, depth_count):
        greet(place(row, col, lax.rem(depth + step, depth_count)))

    @pl.when(has_partner)
    def _():
        source_row = lax.rem(row + col - midpoint + row_count, row_count)
        for step in range(col_count):
            greet(place(source_row, lax.rem(col + step, col_count), depth))

    pl.semaphore_wait(barrier, 2 * (col_count - 1) + depth_count - 1)

    def home_device(step):
        return place(row, lax.rem(col + step, col_count), depth)

    def partner_device(step):
        target_col = lax.rem(col + step, col_count)
        target_row = lax.rem(row + midpoint - target_col + row_count, row_count)
        return place(target_row, target_col, depth)

    def depth_device(step):
        return place(row, col, lax.rem(depth + step, depth_count))

    def send(source, target, send_sem, recv_sem, device):
        return pltpu.make_async_remote_copy(
            src_ref=source, dst_ref=target, send_sem=send_sem, recv_sem=recv_sem,
            device_id=device, device_id_type=MESH,
        )

    def home_copy(step):
        return send(
            x_ref.at[0], home.at[step],
            home_send.at[step], home_recv.at[step], home_device(step),
        )

    def home_rows_copy(step):
        return send(
            rows_hbm.at[0], home_rows.at[step],
            row_send.at[0, step], row_recv.at[0, step], home_device(step),
        )

    def partner_copy(step, chunk):
        return send(
            x_ref.at[0, :, :, pl.ds(chunk * sub, sub)], partner[chunk].at[step],
            partner_send.at[step, chunk], partner_recv.at[step, chunk],
            partner_device(step),
        )

    def partner_rows_copy(step):
        return send(
            rows_hbm.at[0], partner_rows.at[step],
            row_send.at[1, step], row_recv.at[1, step], partner_device(step),
        )

    def pos_copy(step):
        return send(
            pos_vmem.at[0], pos_vmem.at[step],
            pos_send.at[step], pos_recv.at[step], depth_device(step),
        )

    def sum_copy(step, chunk):
        columns = pl.ds(chunk * sub, sub)
        return send(
            send_parts.at[step, columns], recv_parts.at[step, columns],
            sum_send.at[step, chunk], sum_recv.at[step, chunk], depth_device(step),
        )

    def sends_partner(step):
        return lax.rem(col + step, col_count) != midpoint

    for step in range(col_count):
        pl.when(sends_partner(step))(lambda: partner_copy(step, 0).start())
    loads[2].wait()
    for step in range(1, depth_count):
        pos_copy(step).start()
    for step in range(col_count):
        if step:
            home_rows_copy(step).start()
            home_copy(step).start()
        pl.when(sends_partner(step))(lambda: partner_rows_copy(step).start())
    for chunk in range(1, chunks):
        for step in range(col_count):
            pl.when(sends_partner(step))(lambda: partner_copy(step, chunk).start())

    for copy in loads[:2]:
        copy.wait()
    for step in range(1, col_count):
        home_rows_copy(step).wait_recv()
    to_smem = pltpu.make_async_copy(home_rows, rows_smem.at[0], local_sem.at[3])
    to_smem.start()
    for step in range(1, depth_count):
        pos_copy(step).wait_recv()
    positions = [
        pos_vmem[(depth_count - step) % depth_count, 0, 0] for step in range(depth_count)
    ]
    to_smem.wait()
    for step in range(1, col_count):
        home_copy(step).wait_recv()

    def pick(side, read, index, block_row):
        found_blocks = []
        for column in range(width):
            slot = jnp.int32(0)
            found = jnp.int32(0)
            for number in range(slots):
                match = rows_smem[side, index, column, number] == block_row
                slot = jnp.where(match, number, slot)
                found = jnp.where(match, 1, found)
            block = read(index, column, slot)
            found_blocks.append(jnp.where(found > 0, block, jnp.zeros_like(block)))
        return jnp.concatenate(found_blocks, axis=1)

    steps = list(range(1, depth_count)) + [0]
    for step in steps:
        for index in range(col_count):
            left[step, index] = pick(
                0, lambda at, column, slot: home[at, column, slot],
                index, lax.div(positions[step], group_rows),
            )

    def tile(side, read, chunk):
        columns = slice(chunk * sub, (chunk + 1) * sub)
        for step in steps:
            right_row = lax.rem(positions[step], group_rows)
            total = jnp.zeros((sub, size), jnp.float32)
            for index in range(col_count):
                total = total + product(pick(side, read, index, right_row), left[step, index])
            send_parts[step, columns] = total
            if step:
                sum_copy(step, chunk).start()

    @pl.when(has_partner)
    def _():
        for step in range(col_count):
            partner_rows_copy(step).wait_recv()
        moved = pltpu.make_async_copy(partner_rows, rows_smem.at[1], local_sem.at[4])
        moved.start()
        moved.wait()
        for chunk in range(chunks):
            for step in range(col_count):
                partner_copy(step, chunk).wait_recv()
            tile(1, lambda at, column, slot: partner[chunk][at, column, slot], chunk)

    @pl.when(jnp.logical_not(has_partner))
    def _():
        for chunk in range(chunks):
            columns = slice(chunk * sub, (chunk + 1) * sub)
            tile(0, lambda at, column, slot: home[at, column, slot, columns], chunk)

    for chunk in range(chunks):
        columns = slice(chunk * sub, (chunk + 1) * sub)
        total = send_parts[0, columns]
        for step in range(1, depth_count):
            sum_copy(step, chunk).wait_recv()
            total = total + recv_parts[step, columns]
        send_parts[0, columns] = total
    out_ref[0, 0, 0] = send_parts[0].T.astype(out_ref.dtype)

    for step in range(col_count):
        if step:
            home_copy(step).wait_send()
            home_rows_copy(step).wait_send()
        pl.when(sends_partner(step))(lambda: partner_rows_copy(step).wait_send())
    for step in range(1, depth_count):
        pos_copy(step).wait_send()
    for chunk in range(chunks):
        for step in range(col_count):
            pl.when(sends_partner(step))(lambda: partner_copy(step, chunk).wait_send())
        for step in range(1, depth_count):
            sum_copy(step, chunk).wait_send()


def on_device(sizes, x_vals, x_rows, out_block):
    row_count, col_count, depth_count = sizes
    _, width, slots, size, _ = x_vals.shape
    sub = size // CHUNKS
    block_set = (col_count, width, slots)
    dma = pltpu.SemaphoreType.DMA
    return pl.pallas_call(
        functools.partial(kernel, sizes),
        out_shape=jax.ShapeDtypeStruct(out_block.shape + (size, size), jnp.bfloat16),
        in_specs=[
            pl.BlockSpec(memory_space=pl.ANY),
            pl.BlockSpec(memory_space=pl.ANY),
            pl.BlockSpec(memory_space=pl.ANY),
        ],
        out_specs=pl.BlockSpec(memory_space=pltpu.VMEM),
        scratch_shapes=[
            pltpu.VMEM(block_set + (size, size), x_vals.dtype),
            pltpu.VMEM(block_set, jnp.int32),
            tuple(pltpu.VMEM(block_set + (sub, size), x_vals.dtype) for _ in range(CHUNKS)),
            pltpu.VMEM(block_set, jnp.int32),
            pltpu.SMEM((2,) + block_set, jnp.int32),
            pltpu.VMEM((depth_count,) + out_block.shape[1:], jnp.int32),
            pltpu.VMEM((depth_count, col_count, size, width * size), x_vals.dtype),
            pltpu.VMEM((depth_count, size, size), jnp.float32),
            pltpu.VMEM((depth_count, size, size), jnp.float32),
            dma((5,)),
            dma((col_count,)),
            dma((col_count,)),
            dma((col_count, CHUNKS)),
            dma((col_count, CHUNKS)),
            dma((2, col_count)),
            dma((2, col_count)),
            dma((depth_count,)),
            dma((depth_count,)),
            dma((depth_count, CHUNKS)),
            dma((depth_count, CHUNKS)),
        ],
        compiler_params=pltpu.CompilerParams(
            collective_id=0, has_side_effects=True, vmem_limit_bytes=VMEM_LIMIT
        ),
    )(x_rows, out_block, x_vals)


def solution(mesh):
    sizes = tuple(mesh.shape[name] for name in ("row", "col", "depth"))
    in_specs = (
        P("row", ("col", "depth"), None, None, None),
        P("row", ("col", "depth"), None),
        P("row", "col", "depth"),
    )
    out_specs = P("row", "col", "depth", None, None)
    return jax.shard_map(
        functools.partial(on_device, sizes),
        mesh=mesh, in_specs=in_specs, out_specs=out_specs, check_vma=False,
    )
```

profile of v0, /device:TPU:0, one launch (start us, length us, event | category | flops | bytes accessed | tf_op | source)
XLA Modules:
  0.0 20.3 jit_solution(9367983919323245666)
XLA Ops:
  0.7 18.3 %shard_map.37 = bf16[1,1,1,128,128]{4,3,2,1,0:T(8,128)(2,1)} custom-call(s32[1,2,4]{2,1,0:T(2,128)} %rows_hbm.1, s32[1,1,1]{2,1,0:T(1,128)S(6)} %copy.5.pos_ref, bf16[1,2,4,128,128]{4,3,2,1,0:T(8,128)(2,1)} %x_ref.1), custom_call_target="tpu_custom_call" | custom-call | tf_op jit(solution)/shard_map/pallas_call | solution.py:231
  18.9 1.4 %copy.6 = bf16[1,1,1,128,128]{4,3,2,1,0:T(8,128)(2,1)} copy(bf16[1,1,1,128,128]{4,3,2,1,0:T(8,128)(2,1)} %shard_map.37) | data formatting | bytes 65536
where the time goes:
time: 20.5 us; the launch traced here: 20.3 us
  Pallas kernels  18.3 us (89%)
  local copies, waits for them, and re-layouts  1.38 us (7%)
  between operations  0.66 us (3%)
    pallas_call x1, Pallas kernels, on_device(): pl.pallas_call(functools.partial(kernel, sizes), out_shape=jax.ShapeDtype...  18.3 us
    unnamed x1, local copies, waits for them, and re-layouts  1.38 us

commit v1 on v0

--- a/solution.py
+++ b/solution.py
@@ -149,37 +149,43 @@
     for step in range(1, col_count):
         home_copy(step).wait_recv()
 
-    def pick(side, read, index, block_row):
-        found_blocks = []
-        for column in range(width):
-            slot = jnp.int32(0)
-            found = jnp.int32(0)
-            for number in range(slots):
-                match = rows_smem[side, index, column, number] == block_row
-                slot = jnp.where(match, number, slot)
-                found = jnp.where(match, 1, found)
+    def find(side, block_row):
+        places = []
+        for index in range(col_count):
+            for column in range(width):
+                slot = jnp.int32(0)
+                found = jnp.int32(0)
+                for number in range(slots):
+                    match = rows_smem[side, index, column, number] == block_row
+                    slot = jnp.where(match, number, slot)
+                    found = jnp.where(match, 1, found)
+                places.append((index, column, slot, found))
+        return places
+
+    def pick(places, read):
+        blocks = []
+        for index, column, slot, found in places:
             block = read(index, column, slot)
-            found_blocks.append(jnp.where(found > 0, block, jnp.zeros_like(block)))
-        return jnp.concatenate(found_blocks, axis=1)
+            blocks.append(jnp.where(found > 0, block, jnp.zeros_like(block)))
+        return jnp.concatenate(blocks, axis=1)
 
     steps = list(range(1, depth_count)) + [0]
     for step in steps:
-        for index in range(col_count):
-            left[step, index] = pick(
-                0, lambda at, column, slot: home[at, column, slot],
-                index, lax.div(positions[step], group_rows),
-            )
-
-    def tile(side, read, chunk):
+        left[step] = pick(
+            find(0, lax.div(positions[step], group_rows)),
+            lambda index, column, slot: home[index, column, slot],
+        )
+
+    def find_all(side):
+        return [find(side, lax.rem(positions[step], group_rows)) for step in range(depth_count)]
+
+    def tile(places, read, chunk):
         columns = slice(chunk * sub, (chunk + 1) * sub)
-        for step in steps:
-            right_row = lax.rem(positions[step], group_rows)
-            total = jnp.zeros((sub, size), jnp.float32)
-            for index in range(col_count):
-                total = total + product(pick(side, read, index, right_row), left[step, index])
+        totals = [product(pick(places[step], read), left[step]) for step in steps]
+        for step, total in zip(steps, totals):
             send_parts[step, columns] = total
-            if step:
-                sum_copy(step, chunk).start()
+        for step in range(1, depth_count):
+            sum_copy(step, chunk).start()
 
     @pl.when(has_partner)
     def _():
@@ -188,16 +194,18 @@
         moved = pltpu.make_async_copy(partner_rows, rows_smem.at[1], local_sem.at[4])
         moved.start()
         moved.wait()
+        places = find_all(1)
         for chunk in range(chunks):
             for step in range(col_count):
                 partner_copy(step, chunk).wait_recv()
-            tile(1, lambda at, column, slot: partner[chunk][at, column, slot], chunk)
+            tile(places, lambda at, column, slot: partner[chunk][at, column, slot], chunk)
 
     @pl.when(jnp.logical_not(has_partner))
     def _():
+        places = find_all(0)
         for chunk in range(chunks):
             columns = slice(chunk * sub, (chunk + 1) * sub)
-            tile(0, lambda at, column, slot: home[at, column, slot, columns], chunk)
+            tile(places, lambda at, column, slot: home[at, column, slot, columns], chunk)
 
     for chunk in range(chunks):
         columns = slice(chunk * sub, (chunk + 1) * sub)
@@ -244,7 +252,7 @@
             pltpu.VMEM(block_set, jnp.int32),
             pltpu.SMEM((2,) + block_set, jnp.int32),
             pltpu.VMEM((depth_count,) + out_block.shape[1:], jnp.int32),
-            pltpu.VMEM((depth_count, col_count, size, width * size), x_vals.dtype),
+            pltpu.VMEM((depth_count, size, col_count * width * size), x_vals.dtype),
             pltpu.VMEM((depth_count, size, size), jnp.float32),
             pltpu.VMEM((depth_count, size, size), jnp.float32),
             dma((5,)),

time: 20.5 us -> 20.5 us (level)
  no operation moved by 1% of the time
where the time goes in v1:
time: 20.5 us; the launch traced here: 20.3 us
  Pallas kernels  18.3 us (89%)
  local copies, waits for them, and re-layouts  1.38 us (7%)
  between operations  0.66 us (3%)
    pallas_call x1, Pallas kernels, on_device(): pl.pallas_call(functools.partial(kernel, sizes), out_shape=jax.ShapeDtype...  18.3 us
    unnamed x1, local copies, waits for them, and re-layouts  1.38 us

profile of v1, /device:TPU:0, one launch (start us, length us, event | category | flops | bytes accessed | tf_op | source)
XLA Modules:
  0.0 20.3 jit_solution(13501731788131362942)
XLA Ops:
  0.7 18.3 %shard_map.37 = bf16[1,1,1,128,128]{4,3,2,1,0:T(8,128)(2,1)} custom-call(s32[1,2,4]{2,1,0:T(2,128)} %rows_hbm.1, s32[1,1,1]{2,1,0:T(1,128)S(6)} %copy.5.pos_ref, bf16[1,2,4,128,128]{4,3,2,1,0:T(8,128)(2,1)} %x_ref.1), custom_call_target="tpu_custom_call" | custom-call | tf_op jit(solution)/shard_map/pallas_call | solution.py:239
  19.0 1.4 %copy.6 = bf16[1,1,1,128,128]{4,3,2,1,0:T(8,128)(2,1)} copy(bf16[1,1,1,128,128]{4,3,2,1,0:T(8,128)(2,1)} %shard_map.37) | data formatting | bytes 65536
